TPU v7x, 32 devices: a whole 2x2x4 slice. The times are simulated.
32 devices in a mesh: stn: 16 (over z, y, core), tm: 2 (over x).
Axes of the slice: x: 2, y: 2, z: 4, core: 2. Of those that a mesh axis runs over, the one named last changes fastest.
Arguments:
- voltages: bfloat16 [2, 1024, 131072], P(None, 'stn', 'tm'), may hold values from -6 to 6
- filter_taps: float32 [16, 4096], replicated, may hold values from -1.5 to 1.5
- membership: int32 [32, 512], P('stn'), may hold values from 0 to 3
- block_active: int32 [32, 10], P('stn'), may hold values 0 or 1
Outputs:
- visibilities: float32 [32, 10, 2, 256, 256], P('stn', None, None, 'tm')
All inputs are finite; a program needn't handle non-finite values. No bound on the sum of `block_active` on one device may be relied on, other than what follows from the above.
Results may differ from a plain program's by a relative error of at most 0.006.
Values may be sent and summed in bfloat16 or wider, within the bound.
A program may use at most 256 MiB of HBM per device.

v0:
```python
import math

import jax
import jax.numpy as jnp
import numpy as np
from jax import lax
from jax.sharding import PartitionSpec as P

TAPS = 16
RADIX = 64
FFT = 4096
AVG = 16
CH_DEV = 2
F_DEV = 16


def passed_along(shard, axis, by):
    devices = lax.axis_size(axis)
    pairs = [(i, i + by) for i in range(devices) if 0 <= i + by < devices]
    return lax.ppermute(shard, axis, pairs)


def pair_tables(count):
    upper_list = []
    lower_list = []
    for upper in range(count):
        for lower in range(upper + 1):
            upper_list.append(upper)
            lower_list.append(lower)
    return (np.array(upper_list, dtype=np.int32), np.array(lower_list, dtype=np.int32))


def rotation(numer, denom):
    angle = -2.0 * math.pi * numer.astype(jnp.float32) / denom
    return (jnp.cos(angle), jnp.sin(angle))


def complex_table(cosine, sine):
    upper_rows = jnp.stack([cosine, sine], axis=1)
    lower_rows = jnp.stack([-sine, cosine], axis=1)
    return jnp.stack([upper_rows, lower_rows])


def apply_filter(padded, filter_taps, frame_count):
    filtered = filter_taps[0] * padded[:, :, 0:frame_count, :].astype(jnp.float32)
    for tap_index in range(1, TAPS):
        filtered = filtered + filter_taps[tap_index] * padded[
            :, :, tap_index : tap_index + frame_count, :
        ].astype(jnp.float32)
    return filtered


def transform(filtered):
    local_inputs = filtered.shape[1]
    frame_count = filtered.shape[2]
    frame_grid = filtered.reshape(2, local_inputs, frame_count, RADIX, RADIX)
    counter = lax.iota(jnp.int32, RADIX)
    cosine_one, sine_one = rotation(counter[:, None] * counter[None, :] % RADIX, RADIX)
    section_one = jnp.einsum(
        "cifab,cadk->difbk",
        frame_grid,
        complex_table(cosine_one, sine_one),
        precision=lax.Precision.HIGHEST,
    )
    cosine_two, sine_two = rotation(counter[:, None] * counter[None, :], FFT)
    turned = jnp.stack(
        [
            section_one[0] * cosine_two - section_one[1] * sine_two,
            section_one[0] * sine_two + section_one[1] * cosine_two,
        ]
    )
    station_devices = lax.axis_size("stn")
    per_device = CH_DEV * AVG
    pick_count = station_devices * per_device // RADIX
    chosen = (lax.iota(jnp.int32, pick_count) - pick_count // 2) % RADIX
    cosine_three, sine_three = rotation(counter[:, None] * chosen[None, :] % RADIX, RADIX)
    second_table = complex_table(cosine_three, sine_three) / RADIX
    shaped = turned.reshape(2, local_inputs, frame_count, RADIX, RADIX // per_device, per_device)
    return jnp.einsum("cifbhl,cbdj->dijhfl", shaped, second_table, precision=lax.Precision.HIGHEST)


def channelize(voltages, filter_taps):
    local_inputs = voltages.shape[1]
    station_devices = lax.axis_size("stn")
    per_device = CH_DEV * AVG
    own_frames = voltages.reshape(2, local_inputs, F_DEV, FFT)
    tail_frames = own_frames[:, :, F_DEV - TAPS + 1 :, :]
    history_frames = passed_along(tail_frames, "tm", 1)
    padded = jnp.concatenate([history_frames, own_frames], axis=2)
    spectrum = transform(apply_filter(padded, filter_taps, F_DEV))
    return spectrum.reshape(2, local_inputs, station_devices, F_DEV * per_device).astype(
        jnp.bfloat16
    )


def shards(voltages, filter_taps, membership, block_active):
    spectrum = channelize(voltages, filter_taps)
    gathered = lax.all_to_all(spectrum, "stn", split_axis=2, concat_axis=1, tiled=True)
    inputs_all = gathered.shape[1]
    block_size = inputs_all // 4
    upper_tab, lower_tab = pair_tables(4)
    time_devices = lax.axis_size("tm")
    scale = 1.0 / (AVG * F_DEV * time_devices)
    arranged = gathered.reshape(2, inputs_all, F_DEV, CH_DEV, AVG)
    results = []
    for channel in range(CH_DEV):
        samples = arranged[:, :, :, channel, :].reshape(2, inputs_all, F_DEV * AVG)
        left = jnp.concatenate([samples[0], samples[1]], axis=1)
        swapped = jnp.concatenate([samples[1], -samples[0]], axis=1)
        both_sides = jnp.stack([left, swapped])
        flags = block_active[channel]
        rows_left = both_sides.reshape(2, 4, block_size, -1)[:, upper_tab]
        rows_right = left.reshape(4, block_size, -1)[lower_tab]
        product = jnp.einsum(
            "cpik,pjk->pcij", rows_left, rows_right, preferred_element_type=jnp.float32
        )
        station_ids = jnp.repeat(membership[channel], 2).reshape(4, block_size)
        same = (station_ids[upper_tab][:, :, None] == station_ids[lower_tab][:, None, :]).astype(
            jnp.float32
        )
        weight = same * flags.astype(jnp.float32)[:, None, None]
        results.append(product * scale * weight[:, None])
    partial_value = jnp.stack(results)
    return lax.psum_scatter(
        partial_value.astype(jnp.bfloat16), "tm", scatter_dimension=3, tiled=True
    ).astype(jnp.float32)


def solution(mesh):
    placed = (P(None, "stn", "tm"), P(), P("stn", None), P("stn", None))
    return jax.shard_map(
        shards,
        mesh=mesh,
        in_specs=placed,
        out_specs=P("stn", None, None, "tm", None),
        check_vma=False,
    )
```

profile of v0, /device:TPU:14, one launch (start us, length us, event | category | flops | bytes accessed | tf_op | source)
XLA Modules:
  0.0 1102.0 jit_solution(3799909787773434664)
XLA Ops:
  6.5 14.7 %copy.122 = bf16[16,8,16,4096]{3,2,1,0:T(8,128)(2,1)S(1)} copy(bf16[16,8,16,4096]{3,1,2,0:T(8,128)(2,1)} %bitcast.166) | data formatting | bytes 33554432
  21.2 4.7 slice.200
  25.9 1.1 copy-done
  26.9 10.8 copy.90
  37.8 1.8 collective-permute-start
  39.7 0.6 maximum_bitcast_fusion.8
  41.1 338.3 %collective-permute-done = bf16[2,64,15,4096]{3,1,2,0:T(8,128)(2,1)S(1)} collective-permute-done((bf16[2,64,15,4096]{3,1,2,0:T(8,128)(2,1)}, bf16[2,64,15,4096]{3,1,2,0:T(8,128)(2,1)S(1)}, u32[]{:S(2)}, u32[]{:S(2)}) %collective-permute-start) | collective-permute-done | bytes 15728672 | tf_op jit(solution)/shard_map/ppermute | solution.py:20
  379.4 25.7 %copy.91 = bf16[2,64,15,4096]{3,2,1,0:T(8,128)(2,1)} copy(bf16[2,64,15,4096]{3,1,2,0:T(8,128)(2,1)S(1)} %collective-permute-done) | data formatting | bytes 31457280 | tf_op jit(solution)/shard_map/ppermute | solution.py:20
  405.0 188.2 %multiply_add_fusion.1 = f32[2,64,16,4096]{3,2,1,0:T(8,128)} fusion(bf16[2,64,16,4096]{3,2,1,0:T(8,128)(2,1)} %bitcast.161, bf16[2,64,15,4096]{3,2,1,0:T(8,128)(2,1)} %copy.91, f32[4096]{0:T(1024)S(1)} %bitcast.185, f32[4096]{0:T(1024)S(1)} %bitcast.186, f32[4096]{0:T(1024)S(1)} %bitcast.172, f32[4096]{0:T(1024)S(1)} %bitcast.173, f32[4096]{0:T(1024)S(1)} %bitcast.174, ...), kind=kLoop, calls=%fused_computation.45 | loop fusion | flops 771751936 | bytes 66322432 | tf_op jit(solution)/shard_map/add | solution.py:47
  593.2 52.6 %reshape.346 = f32[2,64,16,64,64]{4,3,2,1,0:T(8,128)} reshape(f32[2,64,16,4096]{3,2,1,0:T(8,128)} %multiply_add_fusion.1) | data formatting | bytes 67108864 | tf_op jit(solution)/shard_map/reshape | solution.py:56
  645.9 69.6 %fusion.6 = f32[2,64,16,64,64]{3,4,2,1,0:T(8,128)} fusion(f32[2,64,16,64,64]{4,3,2,1,0:T(8,128)} %reshape.346, f32[2,64,2,64,1,1]{1,3,0,5,4,2:T(8,128)S(1)} %maximum_bitcast_fusion.15), kind=kOutput, calls=%fused_computation.46 | convolution fusion | flops 12884901888 | bytes 67174400 | tf_op jit(solution)/shard_map/cifab,cadk->difbk/dot_general | solution.py:59
  715.5 44.8 %multiply_subtract_fusion = (f32[1,64,16,64,64]{3,4,2,1,0:T(8,128)}, f32[1,64,16,64,64]{3,4,2,1,0:T(8,128)}) fusion(f32[2,64,16,64,64]{3,4,2,1,0:T(8,128)} %fusion.6, f32[64,64]{0,1:T(8,128)S(1)} %get-tuple-element.42, f32[64,64]{0,1:T(8,128)S(1)} %get-tuple-element.43), kind=kLoop, calls=%fused_computation.44 | loop fusion | flops 25165824 | bytes 67141632 | tf_op jit(solution)/shard_map/sub | solution.py:68
  760.3 35.4 %copy.93 = f32[1,64,16,64,2,32]{3,1,0,5,4,2:T(8,128)} copy(f32[1,64,16,64,2,32]{3,5,4,2,1,0:T(8,128)} %bitcast.165) | data formatting | bytes 33554432 | tf_op jit(solution)/shard_map/stack | solution.py:66
  795.8 21.6 %copy.94 = f32[1,64,16,64,2,32]{3,1,0,5,4,2:T(8,128)} copy(f32[1,64,16,64,2,32]{3,5,4,2,1,0:T(8,128)S(1)} %bitcast.164) | data formatting | bytes 33554432 | tf_op jit(solution)/shard_map/stack | solution.py:66
  817.4 84.2 %fusion.27 = bf16[2,64,8,2,16,32]{1,2,5,3,4,0:T(8,128)(2,1)S(1)} fusion(f32[1,64,16,64,2,32]{3,1,0,5,4,2:T(8,128)} %copy.94, f32[1,64,16,64,2,32]{3,1,0,5,4,2:T(8,128)} %copy.93, f32[1,64,2,8]{1,3,0,2:T(8,128)S(1)} %copy-done.4, f32[1,64,2,8]{1,3,0,2:T(8,128)S(1)} %copy-done.3), kind=kOutput, calls=%fused_computation.70 | convolution fusion | flops 1620054016 | bytes 35659776 | tf_op jit(solution)/shard_map/cifbhl,cbdj->dijhfl/dot_general | solution.py:79
  901.7 3.0 copy.95
  904.6 4.8 copy.96
  909.4 6.2 all-to-all-start
  918.5 3.6 select_multiply_fusion
  922.1 40.8 %all-to-all-done = bf16[2,64,16,512]{3,1,0,2:T(8,128)(2,1)S(1)} async-done(((bf16[2,64,16,512]{3,1,0,2:T(8,128)(2,1)}), bf16[2,64,16,512]{3,1,0,2:T(8,128)(2,1)S(1)}, u32[]{:S(2)}, u32[]{:S(2)}) %all-to-all-start) | async-done | bytes 2097184 | tf_op jit(solution)/shard_map/all_to_all | solution.py:98
  962.9 4.7 copy.97
  967.6 5.5 reshape.347
  973.1 1.2 fusion.71
  974.3 1.4 concatenate.45
  975.7 2.2 concatenate.49
  978.0 1.4 concatenate.46
  979.4 2.2 concatenate.50
  981.6 1.2 concatenate.52
  982.8 1.2 concatenate.56
  984.0 1.2 concatenate.53
  985.1 1.1 concatenate.57
  986.7 1.1 copy.99
  987.9 1.4 maximum_maximum_fusion
  989.3 3.8 gather_fusion
  993.1 1.3 copy.102
  994.4 1.3 copy.103
  995.8 2.5 gather_fusion.1
  998.7 2.1 copy.108
  1000.9 1.4 maximum_maximum_fusion.1
  1002.2 4.0 gather_fusion.4
  1006.2 1.3 copy.111
  1007.5 1.3 copy.112
  1009.0 2.3 gather_fusion.5
  1011.3 5.6 fusion.28
  1016.9 5.6 fusion.29
  1022.5 2.8 pad_maximum_fusion.1
  1025.3 64.8 %reduce-scatter.2.cloned.1.call-done = bf16[2,10,2,128,256]{4,3,2,1,0:T(8,128)(2,1)} async-done(((bf16[2,10,2,256,256]{4,3,2,1,0:T(8,128)(2,1)}), bf16[2,10,2,128,256]{4,3,2,1,0:T(8,128)(2,1)}) %reduce-scatter.2.cloned.1.call-update) | async-done | bytes 2621456 | tf_op jit(solution)/shard_map/reduce_scatter | solution.py:124
  1090.2 4.8 convert_element_type.173
  (64 shorter events, 4.7 us)
Async XLA Ops:
  21.2 5.7 copy-start
  26.9 13.9 %copy-start.2 = (f32[16,4096]{1,0:T(8,128)S(1)}, f32[16,4096]{1,0:T(8,128)}, u32[]{:S(2)}) copy-start(f32[16,4096]{1,0:T(8,128)} %param.15) | copy-start | bytes 786436
  37.8 341.6 %collective-permute-start = (bf16[2,64,15,4096]{3,1,2,0:T(8,128)(2,1)}, bf16[2,64,15,4096]{3,1,2,0:T(8,128)(2,1)S(1)}, u32[]{:S(2)}, u32[]{:S(2)}) collective-permute-start(bf16[2,64,15,4096]{3,1,2,0:T(8,128)(2,1)} %copy.90), channel_id=1, source_target_pairs={{0,1},{2,3},{4,5},{6,7},{8,9},{10,11},{12,13},{14,15},{16,17},{18,... | collective-permute-start | bytes 47185928 | tf_op jit(solution)/shard_map/ppermute | solution.py:20
  760.3 35.5 %slice-start = ((s8[33554432]{0:T(1024)(128)(4,1)}), s8[4194304]{0:T(1024)(128)(4,1)S(1)}, s32[]{:S(2)}) async-start(s8[33554432]{0:T(1024)(128)(4,1)} %bitcast.162), calls=%async_computation.3 | async-start | bytes 8388608
  760.3 35.5 %slice-start.1 = ((s8[33554432]{0:T(1024)(128)(4,1)}), s8[4194304]{0:T(1024)(128)(4,1)S(1)}, s32[]{:S(2)}) async-start(s8[33554432]{0:T(1024)(128)(4,1)} %bitcast.162), calls=%async_computation.4 | async-start | bytes 8388608
  760.3 35.5 %slice-start.2 = ((s8[33554432]{0:T(1024)(128)(4,1)}), s8[4194304]{0:T(1024)(128)(4,1)S(1)}, s32[]{:S(2)}) async-start(s8[33554432]{0:T(1024)(128)(4,1)} %bitcast.162), calls=%async_computation.5 | async-start | bytes 8388608
  760.3 35.5 %slice-start.3 = ((s8[33554432]{0:T(1024)(128)(4,1)}), s8[4194304]{0:T(1024)(128)(4,1)S(1)}, s32[]{:S(2)}) async-start(s8[33554432]{0:T(1024)(128)(4,1)} %bitcast.162), calls=%async_computation.6 | async-start | bytes 8388608
  760.3 35.5 %slice-start.4 = ((s8[33554432]{0:T(1024)(128)(4,1)}), s8[4194304]{0:T(1024)(128)(4,1)S(1)}, s32[]{:S(2)}) async-start(s8[33554432]{0:T(1024)(128)(4,1)} %bitcast.162), calls=%async_computation.7 | async-start | bytes 8388608
  760.3 35.5 %slice-start.5 = ((s8[33554432]{0:T(1024)(128)(4,1)}), s8[4194304]{0:T(1024)(128)(4,1)S(1)}, s32[]{:S(2)}) async-start(s8[33554432]{0:T(1024)(128)(4,1)} %bitcast.162), calls=%async_computation.8 | async-start | bytes 8388608
  760.3 35.5 %slice-start.6 = ((s8[33554432]{0:T(1024)(128)(4,1)}), s8[4194304]{0:T(1024)(128)(4,1)S(1)}, s32[]{:S(2)}) async-start(s8[33554432]{0:T(1024)(128)(4,1)} %bitcast.162), calls=%async_computation.9 | async-start | bytes 8388608
  760.3 35.5 %slice-start.7 = ((s8[33554432]{0:T(1024)(128)(4,1)}), s8[4194304]{0:T(1024)(128)(4,1)S(1)}, s32[]{:S(2)}) async-start(s8[33554432]{0:T(1024)(128)(4,1)} %bitcast.162), calls=%async_computation.10 | async-start | bytes 8388608
  795.8 21.6 %copy-start.3 = (f32[1,64,2,8]{1,3,0,2:T(8,128)S(1)}, f32[1,64,2,8]{1,3,0,2:T(8,128)}, u32[]{:S(2)}) copy-start(f32[1,64,2,8]{1,3,0,2:T(8,128)} %get-tuple-element.31) | copy-start | bytes 12292
  795.8 21.6 %copy-start.4 = (f32[1,64,2,8]{1,3,0,2:T(8,128)S(1)}, f32[1,64,2,8]{1,3,0,2:T(8,128)}, u32[]{:S(2)}) copy-start(f32[1,64,2,8]{1,3,0,2:T(8,128)} %get-tuple-element.32) | copy-start | bytes 12292
  901.6 14.1 %copy-start.5 = (s32[2,512]{1,0:T(2,128)S(1)}, s32[2,512]{1,0:T(2,128)}, u32[]{:S(2)}) copy-start(s32[2,512]{1,0:T(2,128)} %param.16) | copy-start | bytes 12292
  901.6 14.3 %copy-start.7 = (s32[10]{0:T(128)S(1)}, s32[10]{0:T(128)}, u32[]{:S(2)}) copy-start(s32[10]{0:T(128)} %constant.70) | copy-start | bytes 124
  901.6 14.9 %copy-start.8 = (s32[10]{0:T(128)S(1)}, s32[10]{0:T(128)}, u32[]{:S(2)}) copy-start(s32[10]{0:T(128)} %constant.71) | copy-start | bytes 124
  901.6 16.9 %copy-start.6 = (s32[2,10]{1,0:T(2,128)S(1)}, s32[2,10]{1,0:T(2,128)}, u32[]{:S(2)}) copy-start(s32[2,10]{1,0:T(2,128)} %param.17) | copy-start | bytes 244
  909.4 53.5 %all-to-all-start = ((bf16[2,64,16,512]{3,1,0,2:T(8,128)(2,1)}), bf16[2,64,16,512]{3,1,0,2:T(8,128)(2,1)S(1)}, u32[]{:S(2)}, u32[]{:S(2)}) async-start(bf16[2,64,16,512]{3,1,0,2:T(8,128)(2,1)} %copy.96), calls=%async_computation | async-start | bytes 4194304 | tf_op jit(solution)/shard_map/all_to_all | solution.py:98
  915.6 174.5 %reduce-scatter.2.cloned.1.call-start = ((), (), s32[]{:S(2)}) async-start(), calls=%async_computation.2 | async-start | bytes 7864320 | tf_op jit(solution)/shard_map/reduce_scatter | solution.py:124
  989.3 9.0 copy-start.1
Sparse Core Ops, SparseCore 0:
  1025.4 64.6 reduce-scatter.1
where the time goes:
time: 1110 us; the launch traced here: 1100 us
  waiting for transfers between devices  444 us (40%)
  other arithmetic  249 us (22%)
  local copies, waits for them, and re-layouts  222 us (20%)
  matrix products  165 us (15%)
  between operations  14 us (1%)
    ppermute x1, waiting for transfers between devices, passed_along(): return lax.ppermute(shard, axis, pairs)  338 us
    add x1, other arithmetic, apply_filter(): filtered + filter_taps[tap_index] * padded[:, :, tap_index:tap_index + fr...  188 us
    dot_general x1, matrix products, transform(): jnp.einsum('cifbhl,cbdj->dijhfl', shaped, second_table, precision=lax.Pre...  84.2 us
    dot_general x1, matrix products, transform(): jnp.einsum('cifab,cadk->difbk', frame_grid, complex_table(cosine_one, sin...  69.6 us
    reduce_scatter x1, waiting for transfers between devices, shards(): lax.psum_scatter(partial_value.astype(jnp.bfloat16), 'tm', scatter_dimens...  64.8 us
    another operation x2, local copies, waits for them, and re-layouts, transform(): jnp.stack([section_one[0] * cosine_two - section_one[1] * sine_two, secti...  57 us
    reshape x1, local copies, waits for them, and re-layouts, transform(): frame_grid = filtered.reshape(2, local_inputs, frame_count, RADIX, RADIX)  52.6 us
    sub x1, other arithmetic, transform(): section_one[0] * cosine_two - section_one[1] * sine_two  44.8 us
  transfers between devices with their start and end apart: 3, of which 3 were waited for; matrix products, arithmetic and copies ran while one was open for 1% of the time, Pallas kernels for 0%

commit v1 on v0

v1 whole, which is shorter than its diff:
```python
import math

import jax
import jax.numpy as jnp
import numpy as np
from jax import lax
from jax.experimental import pallas as pl
from jax.experimental.pallas import tpu as pltpu
from jax.sharding import PartitionSpec as P

RADIX = 64
AVG = 16
BLOCKS = 4
ROWS = 16
LANES = 128
SPLIT = 4


def dft_table(fft, bins):
    quarter = fft // SPLIT
    count = bins // SPLIT
    n = np.arange(quarter)[:, None]
    parts = []
    for r in range(SPLIT):
        k = SPLIT * np.arange(count)[None, :] + r - bins // 2
        angle = 2.0 * math.pi * ((n * k) % fft) / fft
        c, s = np.cos(angle) / RADIX, np.sin(angle) / RADIX
        parts.append(np.block([[c, -s], [s, c]]))
    return np.stack(parts).astype(np.float32).astype(jnp.bfloat16)


def fir_dft_kernel(taps, frames, fft, v_ref, h_ref, w_ref, own_ref, halo_ref, filt, y_ref):
    quarter = fft // SPLIT
    outs = frames + taps - 1

    def chunk(g, carry):
        base = pl.multiple_of(g * LANES, LANES)
        for c in range(2):
            for q in range(SPLIT):
                at = [
                    pl.multiple_of(j * fft + q * quarter + base, LANES) for j in range(frames)
                ]
                v = [
                    v_ref[c, :, pl.ds(a, LANES)].astype(jnp.float32).reshape(2, 8, LANES)
                    for a in at
                ]
                col = pl.multiple_of(q * quarter + base, LANES)
                h = [h_ref[t, :, pl.ds(col, LANES)][None] for t in range(taps)]
                for m in range(outs):
                    acc = None
                    for j in range(max(0, m - taps + 1), min(frames - 1, m) + 1):
                        term = h[j - m + taps - 1] * v[j]
                        acc = term if acc is None else acc + term
                    filt[c, q, m] = acc.reshape(ROWS, LANES)
        for m in range(outs):
            z = [[filt[c, q, m] for q in range(SPLIT)] for c in range(2)]
            s02 = [z[c][0] + z[c][2] for c in range(2)]
            d02 = [z[c][0] - z[c][2] for c in range(2)]
            s13 = [z[c][1] + z[c][3] for c in range(2)]
            d13 = [z[c][1] - z[c][3] for c in range(2)]
            y = [
                (s02[0] + s13[0], s02[1] + s13[1]),
                (d02[0] + d13[1], d02[1] - d13[0]),
                (s02[0] - s13[0], s02[1] - s13[1]),
                (d02[0] - d13[1], d02[1] + d13[0]),
            ]
            for r in range(SPLIT):
                for c in range(2):
                    y_ref[
                        r,
                        m * ROWS : (m + 1) * ROWS,
                        pl.ds(pl.multiple_of(c * quarter + base, LANES), LANES),
                    ] = y[r][c].astype(jnp.bfloat16)
        return carry

    lax.fori_loop(0, quarter // LANES, chunk, 0)
    width = w_ref.shape[2]

    def transform(r, carry):
        z = jnp.dot(y_ref[r], w_ref[r], preferred_element_type=jnp.float32)
        own_ref[r] = z[: frames * ROWS].reshape(frames, ROWS, width)
        halo_ref[r] = z[frames * ROWS :].reshape(taps - 1, ROWS, width).astype(jnp.bfloat16)
        return carry

    lax.fori_loop(0, SPLIT, transform, 0)


def fir_dft(voltages, filter_taps, bins):
    local_inputs = voltages.shape[1]
    taps, fft = filter_taps.shape
    frames = voltages.shape[2] // fft
    outs = frames + taps - 1
    width = 2 * bins // SPLIT
    spread = jnp.broadcast_to(filter_taps[:, None, :], (taps, 8, fft))
    table = jnp.asarray(dft_table(fft, bins))
    once = pl.Buffered(1)

    def body(*refs):
        fir_dft_kernel(taps, frames, fft, *refs)

    return pl.pallas_call(
        body,
        grid=(local_inputs // ROWS,),
        in_specs=[
            pl.BlockSpec((2, ROWS, frames * fft), lambda i: (0, i, 0)),
            pl.BlockSpec((taps, 8, fft), lambda i: (0, 0, 0), pipeline_mode=once),
            pl.BlockSpec(table.shape, lambda i: (0, 0, 0), pipeline_mode=once),
        ],
        out_specs=[
            pl.BlockSpec((SPLIT, frames, ROWS, width), lambda i: (0, 0, i, 0)),
            pl.BlockSpec((SPLIT, taps - 1, ROWS, width), lambda i: (0, 0, i, 0)),
        ],
        out_shape=[
            jax.ShapeDtypeStruct((SPLIT, frames, local_inputs, width), jnp.float32),
            jax.ShapeDtypeStruct((SPLIT, taps - 1, local_inputs, width), jnp.bfloat16),
        ],
        scratch_shapes=[
            pltpu.VMEM((2, SPLIT, outs, ROWS, LANES), jnp.float32),
            pltpu.VMEM((SPLIT, outs * ROWS, 2 * fft // SPLIT), jnp.bfloat16),
        ],
        compiler_params=pltpu.CompilerParams(vmem_limit_bytes=56 * 2**20),
        cost_estimate=pl.CostEstimate(
            flops=2 * outs * local_inputs * 2 * fft * width,
            bytes_accessed=voltages.size * 2,
            transcendentals=0,
        ),
    )(voltages, spread, table)


def spectra(voltages, filter_taps, channels):
    local_inputs = voltages.shape[1]
    taps = filter_taps.shape[0]
    devices = lax.axis_size("stn")
    bins = devices * channels * AVG
    own, halo = fir_dft(voltages, filter_taps, bins)
    frames = own.shape[1]
    times = lax.axis_size("tm")
    arrived = lax.ppermute(halo, "tm", [(i, i + 1) for i in range(times - 1)])
    head = own[:, : taps - 1] + arrived.astype(jnp.float32)
    spectrum = jnp.concatenate([head, own[:, taps - 1 :]], axis=1).astype(jnp.bfloat16)
    per = AVG // SPLIT
    split = spectrum.reshape(SPLIT, frames, local_inputs, 2, devices, channels, per)
    return split.transpose(3, 2, 4, 5, 1, 0, 6).reshape(
        2, local_inputs, devices, channels * frames * AVG
    )


def shards(voltages, filter_taps, membership, block_active):
    channels = membership.shape[0]
    spectrum = spectra(voltages, filter_taps, channels)
    gathered = lax.all_to_all(spectrum, "stn", split_axis=2, concat_axis=1, tiled=True)
    inputs_all = gathered.shape[1]
    gathered = gathered.reshape(2, inputs_all, -1)
    depth = gathered.shape[2] // channels
    block = inputs_all // BLOCKS
    times = lax.axis_size("tm")
    own = lax.axis_index("tm")
    other = [gathered]
    for step in range(1, times):
        other.append(
            lax.ppermute(gathered, "tm", [(i, (i + step) % times) for i in range(times)])
        )
    rows = block // times
    scale = 1.0 / (depth * times)
    results = []
    for channel in range(channels):
        ids = jnp.repeat(membership[channel], 2)
        mine = lax.dynamic_slice_in_dim(ids.reshape(BLOCKS, block), own * rows, rows, 1)
        flags = block_active[channel].astype(jnp.float32)
        total = [0.0] * (BLOCKS * (BLOCKS + 1) // 2)
        for side in other:
            real, imag = side[:, :, channel * depth : (channel + 1) * depth]
            left = jnp.concatenate([real, imag], axis=1)
            swapped = jnp.concatenate([imag, -real], axis=1)
            both = jnp.stack([left, swapped]).reshape(2, BLOCKS, block, 2 * depth)
            both = lax.dynamic_slice_in_dim(both, own * rows, rows, 2)
            for upper in range(BLOCKS):
                product = lax.dot_general(
                    both[:, upper].reshape(2 * rows, 2 * depth),
                    left[: (upper + 1) * block],
                    (((1,), (1,)), ((), ())),
                    preferred_element_type=jnp.float32,
                ).reshape(2, rows, (upper + 1) * block)
                same = (mine[upper][:, None] == ids[None, : (upper + 1) * block]).astype(
                    jnp.float32
                )
                value = product * (scale * same)
                for lower in range(upper + 1):
                    pair = upper * (upper + 1) // 2 + lower
                    piece = value[:, :, lower * block : (lower + 1) * block] * flags[pair]
                    total[pair] = total[pair] + lax.reduce_precision(piece, 8, 7)
        results.append(jnp.stack(total))
    return jnp.stack(results)


def solution(mesh):
    placed = (P(None, "stn", "tm"), P(), P("stn", None), P("stn", None))
    return jax.shard_map(
        shards,
        mesh=mesh,
        in_specs=placed,
        out_specs=P("stn", None, None, "tm", None),
        check_vma=False,
    )
```

time: 1110 us -> 258 us (0.23)
  waiting for transfers between devices: 444 us -> 127 us
  other arithmetic: 249 us -> 28.1 us
  local copies, waits for them, and re-layouts: 222 us -> 21.4 us
  matrix products: 165 us -> 8.4 us
  Pallas kernels: 0 us -> 64.2 us
  between operations: 14 us -> 0.51 us
    ppermute x1 -> x2, waiting for transfers between devices: 338 us -> 88 us  [the longest x1 44.3 us: spectra(): arrived = lax.ppermute(halo, 'tm', [(i, i + 1) for i in range(times - 1)])]
    add x1 -> x0, other arithmetic: 188 us -> none  [apply_filter(): filtered + filter_taps[tap_index] * padded[:, :, tap_index:tap_index + fr...]
    dot_general x4 -> x16, matrix products: 165 us -> 8.4 us  [shards(): lax.dot_general(both[:, upper].reshape(2 * rows, 2 * depth), left[:(upper...]
    reduce_scatter x1 -> x0, waiting for transfers between devices: 64.8 us -> none  [shards(): lax.psum_scatter(partial_value.astype(jnp.bfloat16), 'tm', scatter_dimens...]
    pallas_call x0 -> x1, Pallas kernels: none -> 64.2 us  [fir_dft(): pl.pallas_call(body, grid=(local_inputs // ROWS,), in_specs=[pl.BlockSpec...]
    another operation x2 -> x3, local copies, waits for them, and re-layouts: 57 us -> 3.6 us  [transform(): jnp.stack([section_one[0] * cosine_two - section_one[1] * sine_two, secti...]
    reshape x2 -> x1, local copies, waits for them, and re-layouts: 58.1 us -> 5.5 us  [spectra(): split.transpose(3, 2, 4, 5, 1, 0, 6)]
    sub x1 -> x0, other arithmetic: 44.8 us -> none  [transform(): section_one[0] * cosine_two - section_one[1] * sine_two]
  transfers between devices with their start and end apart: 3 -> 3, of which waited for: 3 -> 3; matrix products, arithmetic and copies ran while one was open for 1% -> 5% of each run, Pallas kernels for 0% -> 0%
where the time goes in v1:
time: 258 us
  waiting for transfers between devices  127 us (49%)
  Pallas kernels  64.2 us (25%)
  other arithmetic  28.1 us (11%)
  local copies, waits for them, and re-layouts  21.4 us (8%)
  matrix products  8.4 us (3%)
  starting transfers between devices  7.73 us (3%)
    pallas_call x1, Pallas kernels, fir_dft(): pl.pallas_call(body, grid=(local_inputs // ROWS,), in_specs=[pl.BlockSpec...  64.2 us
    ppermute x1, waiting for transfers between devices, spectra(): arrived = lax.ppermute(halo, 'tm', [(i, i + 1) for i in range(times - 1)])  44.3 us
    ppermute x1, waiting for transfers between devices, shards(): lax.ppermute(gathered, 'tm', [(i, (i + step) % times) for i in range(time...  43.7 us
    all_to_all x1, waiting for transfers between devices, shards(): lax.all_to_all(spectrum, 'stn', split_axis=2, concat_axis=1, tiled=True)  39.4 us
    unnamed x16, other arithmetic  10.8 us
    dot_general x16, matrix products, shards(): lax.dot_general(both[:, upper].reshape(2 * rows, 2 * depth), left[:(upper...  8.4 us
    all_to_all x1, starting transfers between devices, shards(): lax.all_to_all(spectrum, 'stn', split_axis=2, concat_axis=1, tiled=True)  6.37 us
    reshape x1, local copies, waits for them, and re-layouts, spectra(): split.transpose(3, 2, 4, 5, 1, 0, 6)  5.5 us
  transfers between devices with their start and end apart: 3, of which 3 were waited for; matrix products, arithmetic and copies ran while one was open for 5% of the time, Pallas kernels for 0%

profile of v1, /device:TPU:14, one launch (start us, length us, event | category | flops | bytes accessed | tf_op | source)
XLA Modules:
  0.0 257.7 jit_solution(2957599205176248427)
XLA Ops:
  0.0 2.5 broadcast_in_dim.30.refs_1_
  2.5 64.2 %shard_map.55 = (f32[4,16,64,256]{3,2,1,0:T(8,128)}, bf16[4,15,64,256]{3,2,1,0:T(8,128)(2,1)}) custom-call(bf16[2,64,65536]{2,1,0:T(8,128)(2,1)} %refs_0_.1, f32[16,8,4096]{2,1,0:T(8,128)} %broadcast_in_dim.30.refs_1_, bf16[4,2048,256]{2,1,0:T(8,128)(2,1)} %constant.26.clone.refs_2_), custom_call_target="tpu_custom_call" | custom-call | flops 8321499136 | bytes 16777216 | tf_op jit(solution)/shard_map/pallas_call | solution.py:101
  66.7 1.3 collective-permute-start
  68.0 1.0 slice.1014
  69.2 44.3 %collective-permute-done = bf16[4,15,64,256]{3,2,1,0:T(8,128)(2,1)} collective-permute-done((bf16[4,15,64,256]{3,2,1,0:T(8,128)(2,1)}, bf16[4,15,64,256]{3,2,1,0:T(8,128)(2,1)}, u32[]{:S(2)}, u32[]{:S(2)}) %collective-permute-start) | collective-permute-done | bytes 1966112 | tf_op jit(solution)/shard_map/ppermute | solution.py:138
  113.5 3.4 %add_convert_fusion = bf16[4,15,64,256]{3,2,1,0:T(8,128)(2,1)S(1)} fusion(bf16[4,15,64,256]{3,2,1,0:T(8,128)(2,1)} %collective-permute-done, f32[4,16,64,256]{3,2,1,0:T(8,128)} %get-tuple-element.7), kind=kLoop, calls=%fused_computation.2 | loop fusion | flops 2949120 | bytes 7864320 | tf_op jit(solution)/shard_map/convert.4
  116.9 3.1 %copy.69 = bf16[4,15,64,256]{2,3,1,0:T(8,128)(2,1)} copy(bf16[4,15,64,256]{3,2,1,0:T(8,128)(2,1)S(1)} %add_convert_fusion) | data formatting | bytes 3932160 | tf_op jit(solution)/shard_map/convert.4
  119.9 5.5 %maximum_bitcast_fusion = bf16[2,64,16,2,16,4,4]{1,6,3,2,0,4,5:T(4,128)(2,1)S(1)} fusion(bf16[4,1,64,2,16,2,4]{2,6,5,4,3,1,0:T(4,128)(2,1)S(1)} %bitcast.290, bf16[4,15,64,2,16,2,4]{2,6,5,4,3,1,0:T(4,128)(2,1)} %bitcast.270), kind=kLoop, calls=%fused_computation.1 | loop fusion | flops 1048576 | bytes 4194304 | tf_op jit(solution)/shard_map/transpose | solution.py:143
  125.4 3.4 %copy.72 = bf16[2,64,16,2,16,4,4]{1,2,6,5,4,3,0:T(8,128)(2,1)} copy(bf16[2,64,16,2,16,4,4]{1,6,3,2,0,4,5:T(4,128)(2,1)S(1)} %maximum_bitcast_fusion) | data formatting | bytes 4194304 | tf_op jit(solution)/shard_map/transpose | solution.py:143
  128.8 5.5 %copy.73 = bf16[2,64,16,512]{3,1,0,2:T(8,128)(2,1)} copy(bf16[2,64,16,512]{1,2,3,0:T(8,128)(2,1)} %bitcast.269) | data formatting | bytes 4194304 | tf_op jit(solution)/shard_map/reshape | solution.py:143
  134.3 6.4 %all-to-all-start = ((bf16[2,64,16,512]{3,1,0,2:T(8,128)(2,1)}), bf16[2,64,16,512]{3,1,0,2:T(8,128)(2,1)S(1)}, u32[]{:S(2)}, u32[]{:S(2)}) async-start(bf16[2,64,16,512]{3,1,0,2:T(8,128)(2,1)} %copy.73), calls=%async_computation | async-start | bytes 4194304 | tf_op jit(solution)/shard_map/all_to_all | solution.py:151
  143.6 0.7 fusion.180
  144.3 0.7 fusion.181
  145.0 0.7 compare_select_fusion.7
  145.8 0.8 compare_select_fusion.5
  146.7 0.9 compare_select_fusion.3
  147.5 0.8 compare_select_fusion.2
  148.6 39.4 %all-to-all-done = bf16[2,64,16,512]{3,1,0,2:T(8,128)(2,1)S(1)} async-done(((bf16[2,64,16,512]{3,1,0,2:T(8,128)(2,1)}), bf16[2,64,16,512]{3,1,0,2:T(8,128)(2,1)S(1)}, u32[]{:S(2)}, u32[]{:S(2)}) %all-to-all-start) | async-done | bytes 2097184 | tf_op jit(solution)/shard_map/all_to_all | solution.py:151
  188.9 0.7 copy-done
  191.4 0.5 convolution_multiply_fusion.3
  191.9 0.5 convolution_multiply_fusion.1
  192.4 43.7 %collective-permute-done.1 = bf16[2,1024,512]{2,1,0:T(8,128)(2,1)S(1)} collective-permute-done((bf16[2,1024,512]{2,1,0:T(8,128)(2,1)S(1)}, bf16[2,1024,512]{2,1,0:T(8,128)(2,1)S(1)}, u32[]{:S(2)}, u32[]{:S(2)}) %collective-permute-start.1) | collective-permute-done | bytes 2097184 | tf_op jit(solution)/shard_map/ppermute | solution.py:161
  237.4 0.5 convolution_multiply_fusion.2
  238.3 0.4 convolution_multiply_fusion.4
  238.7 0.5 convolution_multiply_fusion
  239.2 1.0 fusion.5
  240.1 1.0 fusion.10
  241.1 0.8 fusion.1
  241.9 0.8 fusion.13
  242.8 0.7 fusion.158
  243.5 0.7 fusion.153
  244.1 0.6 fusion.148
  244.7 0.7 fusion.143
  245.4 0.6 fusion.138
  246.0 0.7 fusion.133
  246.7 0.7 fusion.128
  247.4 0.6 fusion.123
  248.1 0.7 fusion.118
  248.8 0.7 fusion.113
  249.5 0.6 fusion.108
  250.1 0.7 fusion.103
  250.8 0.7 fusion.98
  251.6 0.7 fusion.93
  252.3 0.6 fusion.88
  253.0 0.8 fusion.83
  253.7 0.6 fusion.78
  254.3 0.7 fusion.73
  255.0 2.7 %pad_maximum_fusion = f32[2,10,2,128,256]{4,3,2,1,0:T(8,128)} fusion(f32[1,10,2,128,256]{4,3,2,1,0:T(8,128)S(1)} %bitcast.282, f32[1,10,2,128,256]{4,3,2,1,0:T(8,128)S(1)} %bitcast.283), kind=kLoop, calls=%fused_computation | loop fusion | flops 1310720 | bytes 10485760 | tf_op jit(solution)/shard_map/stack | solution.py:193
  (59 shorter events, 7.6 us)
Async XLA Ops:
  66.7 46.8 %collective-permute-start = (bf16[4,15,64,256]{3,2,1,0:T(8,128)(2,1)}, bf16[4,15,64,256]{3,2,1,0:T(8,128)(2,1)}, u32[]{:S(2)}, u32[]{:S(2)}) collective-permute-start(bf16[4,15,64,256]{3,2,1,0:T(8,128)(2,1)} %get-tuple-element.8), channel_id=1, source_target_pairs={{0,1},{2,3},{4,5},{6,7},{8,9},{10,11},{12,13},{14,15},{16,17},{18,... | collective-permute-start | bytes 5898248 | tf_op jit(solution)/shard_map/ppermute | solution.py:138
  134.3 6.4 %copy-start.4 = (s32[2,512]{1,0:T(2,128)S(1)}, s32[2,512]{1,0:T(2,128)}, u32[]{:S(2)}) copy-start(s32[2,512]{1,0:T(2,128)} %param.7) | copy-start | bytes 12292
  134.3 53.6 %all-to-all-start = ((bf16[2,64,16,512]{3,1,0,2:T(8,128)(2,1)}), bf16[2,64,16,512]{3,1,0,2:T(8,128)(2,1)S(1)}, u32[]{:S(2)}, u32[]{:S(2)}) async-start(bf16[2,64,16,512]{3,1,0,2:T(8,128)(2,1)} %copy.73), calls=%async_computation | async-start | bytes 4194304 | tf_op jit(solution)/shard_map/all_to_all | solution.py:151
  140.7 2.9 %copy-start.5 = (s32[2,10]{1,0:T(2,128)S(1)}, s32[2,10]{1,0:T(2,128)}, u32[]{:S(2)}) copy-start(s32[2,10]{1,0:T(2,128)} %param.8) | copy-start | bytes 244
  188.1 47.9 %collective-permute-start.1 = (bf16[2,1024,512]{2,1,0:T(8,128)(2,1)S(1)}, bf16[2,1024,512]{2,1,0:T(8,128)(2,1)S(1)}, u32[]{:S(2)}, u32[]{:S(2)}) collective-permute-start(bf16[2,1024,512]{2,1,0:T(8,128)(2,1)S(1)} %bitcast.271), channel_id=1, source_target_pairs={{0,1},{1,0},{2,3},{3,2},{4,5},{5,4},{6,7},{7,6},{8,9},{9,8},{10,11... | collective-permute-start | bytes 6291464 | tf_op jit(solution)/shard_map/ppermute | solution.py:161
  188.7 1.0 copy-start
  188.9 1.4 copy-start.3
  190.0 1.0 copy-start.2
  238.2 0.9 copy-start.1

commit v2 on v1

--- a/solution.py
+++ b/solution.py
@@ -14,6 +14,7 @@
 ROWS = 16
 LANES = 128
 SPLIT = 4
+PARTS = 2
 
 
 def dft_table(fft, bins):
@@ -85,14 +86,13 @@
     lax.fori_loop(0, SPLIT, transform, 0)
 
 
-def fir_dft(voltages, filter_taps, bins):
-    local_inputs = voltages.shape[1]
-    taps, fft = filter_taps.shape
+def fir_dft(voltages, spread, table, part, parts):
+    local_inputs = voltages.shape[1] // parts
+    taps, _, fft = spread.shape
     frames = voltages.shape[2] // fft
     outs = frames + taps - 1
-    width = 2 * bins // SPLIT
-    spread = jnp.broadcast_to(filter_taps[:, None, :], (taps, 8, fft))
-    table = jnp.asarray(dft_table(fft, bins))
+    width = table.shape[2]
+    steps = local_inputs // ROWS
     once = pl.Buffered(1)
 
     def body(*refs):
@@ -100,9 +100,9 @@
 
     return pl.pallas_call(
         body,
-        grid=(local_inputs // ROWS,),
+        grid=(steps,),
         in_specs=[
-            pl.BlockSpec((2, ROWS, frames * fft), lambda i: (0, i, 0)),
+            pl.BlockSpec((2, ROWS, frames * fft), lambda i: (0, part * steps + i, 0)),
             pl.BlockSpec((taps, 8, fft), lambda i: (0, 0, 0), pipeline_mode=once),
             pl.BlockSpec(table.shape, lambda i: (0, 0, 0), pipeline_mode=once),
         ],
@@ -120,56 +120,58 @@
         ],
         compiler_params=pltpu.CompilerParams(vmem_limit_bytes=56 * 2**20),
         cost_estimate=pl.CostEstimate(
-            flops=2 * outs * local_inputs * 2 * fft * width,
-            bytes_accessed=voltages.size * 2,
+            flops=20 * outs * local_inputs * 2 * fft * width,
+            bytes_accessed=voltages.size * 2 // parts,
             transcendentals=0,
         ),
     )(voltages, spread, table)
 
 
-def spectra(voltages, filter_taps, channels):
-    local_inputs = voltages.shape[1]
-    taps = filter_taps.shape[0]
-    devices = lax.axis_size("stn")
-    bins = devices * channels * AVG
-    own, halo = fir_dft(voltages, filter_taps, bins)
-    frames = own.shape[1]
+def with_history(own, halo):
+    late = halo.shape[1]
     times = lax.axis_size("tm")
     arrived = lax.ppermute(halo, "tm", [(i, i + 1) for i in range(times - 1)])
-    head = own[:, : taps - 1] + arrived.astype(jnp.float32)
-    spectrum = jnp.concatenate([head, own[:, taps - 1 :]], axis=1).astype(jnp.bfloat16)
-    per = AVG // SPLIT
-    split = spectrum.reshape(SPLIT, frames, local_inputs, 2, devices, channels, per)
-    return split.transpose(3, 2, 4, 5, 1, 0, 6).reshape(
-        2, local_inputs, devices, channels * frames * AVG
-    )
+    head = own[:, :late] + arrived.astype(jnp.float32)
+    return jnp.concatenate([head, own[:, late:]], axis=1).astype(jnp.bfloat16)
 
 
 def shards(voltages, filter_taps, membership, block_active):
     channels = membership.shape[0]
-    spectrum = spectra(voltages, filter_taps, channels)
-    gathered = lax.all_to_all(spectrum, "stn", split_axis=2, concat_axis=1, tiled=True)
-    inputs_all = gathered.shape[1]
-    gathered = gathered.reshape(2, inputs_all, -1)
-    depth = gathered.shape[2] // channels
+    devices, times = lax.axis_size("stn"), lax.axis_size("tm")
+    local_inputs = voltages.shape[1]
+    taps, fft = filter_taps.shape
+    spread = jnp.broadcast_to(filter_taps[:, None, :], (taps, 8, fft))
+    table = jnp.asarray(dft_table(fft, devices * channels * AVG))
+    parts = min(PARTS, local_inputs // ROWS)
+    made = [fir_dft(voltages, spread, table, part, parts) for part in range(parts)]
+    spectrum = jnp.concatenate([with_history(*pair) for pair in made], axis=2)
+    frames = spectrum.shape[1]
+    depth = frames * AVG
+    split = spectrum.reshape(
+        SPLIT, frames, local_inputs, 2, devices, channels, AVG // SPLIT
+    ).transpose(3, 2, 4, 5, 1, 0, 6)
+    split = split.reshape(2, local_inputs, devices, channels * depth)
+    landed = lax.all_to_all(split, "stn", split_axis=2, concat_axis=1, tiled=True)
+    inputs_all = local_inputs * devices
     block = inputs_all // BLOCKS
-    times = lax.axis_size("tm")
     own = lax.axis_index("tm")
-    other = [gathered]
-    for step in range(1, times):
-        other.append(
-            lax.ppermute(gathered, "tm", [(i, (i + step) % times) for i in range(times)])
-        )
     rows = block // times
     scale = 1.0 / (depth * times)
     results = []
     for channel in range(channels):
+        gathered = landed[..., channel * depth : (channel + 1) * depth].reshape(
+            2, inputs_all, depth
+        )
+        other = [gathered]
+        for step in range(1, times):
+            around = [(i, (i + step) % times) for i in range(times)]
+            other.append(lax.ppermute(gathered, "tm", around))
         ids = jnp.repeat(membership[channel], 2)
         mine = lax.dynamic_slice_in_dim(ids.reshape(BLOCKS, block), own * rows, rows, 1)
         flags = block_active[channel].astype(jnp.float32)
         total = [0.0] * (BLOCKS * (BLOCKS + 1) // 2)
         for side in other:
-            real, imag = side[:, :, channel * depth : (channel + 1) * depth]
+            real, imag = side
             left = jnp.concatenate([real, imag], axis=1)
             swapped = jnp.concatenate([imag, -real], axis=1)
             both = jnp.stack([left, swapped]).reshape(2, BLOCKS, block, 2 * depth)

time: 258 us -> 246 us (0.953)
  waiting for transfers between devices: 127 us -> 100 us
  Pallas kernels: 64.2 us -> 69.5 us
  local copies, waits for them, and re-layouts: 21.4 us -> 25.2 us
  starting transfers between devices: 7.73 us -> 11.2 us
  other arithmetic: 28.1 us -> 30.9 us
    ppermute x2 -> x4, waiting for transfers between devices: 88 us -> 60.5 us  [the longest x2 41.7 us: shards(): other.append(lax.ppermute(gathered, 'tm', around))]
    pallas_call x1 -> x2, Pallas kernels: 64.2 us -> 69.5 us  [fir_dft(): pl.pallas_call(body, grid=(steps,), in_specs=[pl.BlockSpec((2, ROWS, fram...]
    ppermute x2 -> x4, starting transfers between devices: 1.35 us -> 4.79 us  [the longest x2 2.69 us: with_history(): arrived = lax.ppermute(halo, 'tm', [(i, i + 1) for i in range(times - 1)])]
    transpose x1, other arithmetic: 5.48 us -> 8.52 us  [shards(): split = spectrum.reshape(SPLIT, frames, local_inputs, 2, devices, channel...]
    another operation x3 -> x5, local copies, waits for them, and re-layouts: 3.6 us -> 6.59 us
    reshape x1 -> x2, local copies, waits for them, and re-layouts: 5.5 us -> 5.6 us  [the longest x1 5.46 us: shards(): split = split.reshape(2, local_inputs, devices, channels * depth)]
  transfers between devices with their start and end apart: 3 -> 5, of which waited for: 3 -> 4; matrix products, arithmetic and copies ran while one was open for 5% -> 7% of each run, Pallas kernels for 0% -> 14%
where the time goes in v2:
time: 246 us; the launch traced here: 245 us
  waiting for transfers between devices  100 us (41%)
  Pallas kernels  69.5 us (28%)
  other arithmetic  30.9 us (13%)
  local copies, waits for them, and re-layouts  25.2 us (10%)
  starting transfers between devices  11.2 us (5%)
  matrix products  8.12 us (3%)
    pallas_call x2, Pallas kernels, fir_dft(): pl.pallas_call(body, grid=(steps,), in_specs=[pl.BlockSpec((2, ROWS, fram...  69.5 us
    ppermute x2, waiting for transfers between devices, shards(): other.append(lax.ppermute(gathered, 'tm', around))  41.7 us
    all_to_all x1, waiting for transfers between devices, shards(): lax.all_to_all(split, 'stn', split_axis=2, concat_axis=1, tiled=True)  39.4 us
    ppermute x2, waiting for transfers between devices, with_history(): arrived = lax.ppermute(halo, 'tm', [(i, i + 1) for i in range(times - 1)])  18.8 us
    unnamed x16, other arithmetic  11 us
    transpose x1, other arithmetic, shards(): split = spectrum.reshape(SPLIT, frames, local_inputs, 2, devices, channel...  8.52 us
    dot_general x16, matrix products, shards(): lax.dot_general(both[:, upper].reshape(2 * rows, 2 * depth), left[:(upper...  8.12 us
    all_to_all x1, starting transfers between devices, shards(): lax.all_to_all(split, 'stn', split_axis=2, concat_axis=1, tiled=True)  6.37 us
  transfers between devices with their start and end apart: 5, of which 4 were waited for; matrix products, arithmetic and copies ran while one was open for 7% of the time, Pallas kernels for 14%

profile of v2, /device:TPU:14, one launch (start us, length us, event | category | flops | bytes accessed | tf_op | source)
XLA Modules:
  0.0 245.4 jit_solution(14209534306348838764)
XLA Ops:
  0.0 2.5 %broadcast_in_dim.30.refs_1_ = f32[16,8,4096]{2,1,0:T(8,128)} broadcast(f32[16,4096]{1,0:T(8,128)} %param.6), dimensions={0,2} | broadcast | bytes 2359296 | tf_op jit(solution)/shard_map/broadcast_in_dim | solution.py:143
  2.5 34.7 %shard_map.55 = (f32[4,16,32,256]{3,2,1,0:T(8,128)}, bf16[4,15,32,256]{3,2,1,0:T(8,128)(2,1)}) custom-call(bf16[2,64,65536]{2,1,0:T(8,128)(2,1)} %refs_0_.3, f32[16,8,4096]{2,1,0:T(8,128)} %broadcast_in_dim.30.refs_1_, bf16[4,2048,256]{2,1,0:T(8,128)(2,1)} %constant.26.clone.refs_2_), custom_call_target="tpu_custom_call" | custom-call | flops 41607495680 | bytes 8388608 | tf_op jit(solution)/shard_map/pallas_call | solution.py:101
  37.2 1.4 collective-permute-start
  38.6 34.8 %shard_map.56 = (f32[4,16,32,256]{3,2,1,0:T(8,128)}, bf16[4,15,32,256]{3,2,1,0:T(8,128)(2,1)}) custom-call(bf16[2,64,65536]{2,1,0:T(8,128)(2,1)} %refs_0_.3, f32[16,8,4096]{2,1,0:T(8,128)} %broadcast_in_dim.30.refs_1_, bf16[4,2048,256]{2,1,0:T(8,128)(2,1)} %constant.26.clone.refs_2_), custom_call_target="tpu_custom_call" | custom-call | flops 41607495680 | bytes 8388608 | tf_op jit(solution)/shard_map/pallas_call | solution.py:101
  73.4 1.3 collective-permute-start.1
  74.9 0.9 slice.1034
  75.8 0.9 copy.80
  76.7 1.5 add_convert_fusion.1
  78.2 3.0 %copy.76 = bf16[4,15,32,256]{2,3,1,0:T(8,128)(2,1)} copy(bf16[4,15,32,256]{3,2,1,0:T(8,128)(2,1)S(1)} %add_convert_fusion.1) | data formatting | bytes 1966080 | tf_op jit(solution)/shard_map/convert.9
  81.3 18.8 %collective-permute-done.1 = bf16[4,15,32,256]{3,2,1,0:T(8,128)(2,1)} collective-permute-done((bf16[4,15,32,256]{3,2,1,0:T(8,128)(2,1)}, bf16[4,15,32,256]{3,2,1,0:T(8,128)(2,1)}, u32[]{:S(2)}, u32[]{:S(2)}) %collective-permute-start.1) | collective-permute-done | bytes 983072 | tf_op jit(solution)/shard_map/ppermute | solution.py:133
  100.1 1.5 add_convert_fusion
  101.7 3.0 %copy.79 = bf16[4,15,32,256]{2,3,1,0:T(8,128)(2,1)} copy(bf16[4,15,32,256]{3,2,1,0:T(8,128)(2,1)S(1)} %add_convert_fusion) | data formatting | bytes 1966080 | tf_op jit(solution)/shard_map/convert.4
  104.7 8.5 %maximum_bitcast_fusion = bf16[2,64,16,2,16,4,4]{1,6,3,2,0,4,5:T(4,128)(2,1)S(1)} fusion(bf16[4,1,32,2,16,2,4]{2,6,5,4,3,1,0:T(4,128)(2,1)S(1)} %bitcast.300, bf16[4,15,32,2,16,2,4]{2,6,5,4,3,1,0:T(4,128)(2,1)} %bitcast.281, bf16[4,1,32,2,16,2,4]{2,6,5,4,3,1,0:T(4,128)(2,1)S(1)} %bitcast.299, bf16[4,15,32,2,16,2,4]{2,6,5,4,3,1,0:T(4,128)(2,1)} %bitcast.280), kind=kLoop, calls=%fused_computation.1 | loop fusion | flops 8388608 | bytes 4194304 | tf_op jit(solution)/shard_map/transpose | solution.py:152
  113.2 3.4 %copy.82 = bf16[2,64,16,2,16,4,4]{1,2,6,5,4,3,0:T(8,128)(2,1)} copy(bf16[2,64,16,2,16,4,4]{1,6,3,2,0,4,5:T(4,128)(2,1)S(1)} %maximum_bitcast_fusion) | data formatting | bytes 4194304 | tf_op jit(solution)/shard_map/transpose | solution.py:152
  116.6 5.5 %copy.83 = bf16[2,64,16,512]{3,1,0,2:T(8,128)(2,1)} copy(bf16[2,64,16,512]{1,2,3,0:T(8,128)(2,1)} %bitcast.279) | data formatting | bytes 4194304 | tf_op jit(solution)/shard_map/reshape | solution.py:153
  122.1 6.4 %all-to-all-start = ((bf16[2,64,16,512]{3,1,0,2:T(8,128)(2,1)}), bf16[2,64,16,512]{3,1,0,2:T(8,128)(2,1)S(1)}, u32[]{:S(2)}, u32[]{:S(2)}) async-start(bf16[2,64,16,512]{3,1,0,2:T(8,128)(2,1)} %copy.83), calls=%async_computation | async-start | bytes 4194304 | tf_op jit(solution)/shard_map/all_to_all | solution.py:154
  131.3 0.7 fusion.181
  132.0 0.7 fusion.182
  132.7 0.7 compare_select_fusion.7
  133.5 0.8 compare_select_fusion.5
  134.4 0.9 compare_select_fusion.3
  135.2 0.8 compare_select_fusion.2
  136.3 39.4 %all-to-all-done = bf16[2,64,16,512]{3,1,0,2:T(8,128)(2,1)S(1)} async-done(((bf16[2,64,16,512]{3,1,0,2:T(8,128)(2,1)}), bf16[2,64,16,512]{3,1,0,2:T(8,128)(2,1)S(1)}, u32[]{:S(2)}, u32[]{:S(2)}) %all-to-all-start) | async-done | bytes 2097184 | tf_op jit(solution)/shard_map/all_to_all | solution.py:154
  176.4 2.0 collective-permute-start.3
  182.2 20.1 %collective-permute-done.2 = bf16[2,1024,256]{2,1,0:T(8,128)(2,1)S(1)} collective-permute-done((bf16[2,1024,256]{2,1,0:T(8,128)(2,1)S(1)}, bf16[2,1024,256]{2,1,0:T(8,128)(2,1)S(1)}, u32[]{:S(2)}, u32[]{:S(2)}) %collective-permute-start.2) | collective-permute-done | bytes 1048608 | tf_op jit(solution)/shard_map/ppermute | solution.py:168
  202.6 21.6 %collective-permute-done.3 = bf16[2,1024,256]{2,1,0:T(8,128)(2,1)S(1)} collective-permute-done((bf16[2,1024,256]{2,1,0:T(8,128)(2,1)S(1)}, bf16[2,1024,256]{2,1,0:T(8,128)(2,1)S(1)}, u32[]{:S(2)}, u32[]{:S(2)}) %collective-permute-start.3) | collective-permute-done | bytes 1048608 | tf_op jit(solution)/shard_map/ppermute | solution.py:168
  227.1 0.8 fusion.5
  228.0 0.8 fusion.10
  228.8 0.8 fusion.1
  229.6 0.8 fusion.13
  230.4 0.7 fusion.158
  231.1 0.7 fusion.153
  231.8 0.7 fusion.148
  232.5 0.6 fusion.143
  233.1 0.7 fusion.138
  233.8 0.6 fusion.133
  234.4 0.7 fusion.128
  235.1 0.7 fusion.123
  235.8 0.6 fusion.118
  236.4 0.8 fusion.113
  237.2 0.7 fusion.108
  238.5 0.7 fusion.98
  239.2 0.7 fusion.93
  240.0 0.7 fusion.88
  240.7 0.6 fusion.83
  241.3 0.8 fusion.78
  242.1 0.6 fusion.73
  242.7 2.7 %pad_maximum_fusion = f32[2,10,2,128,256]{4,3,2,1,0:T(8,128)} fusion(f32[1,10,2,128,256]{4,3,2,1,0:T(8,128)S(1)} %bitcast.291, f32[1,10,2,128,256]{4,3,2,1,0:T(8,128)S(1)} %bitcast.292), kind=kLoop, calls=%fused_computation | loop fusion | flops 1310720 | bytes 10485760 | tf_op jit(solution)/shard_map/stack | solution.py:195
  (77 shorter events, 11.3 us)
Async XLA Ops:
  37.2 37.5 %copy-start.2 = (f32[4,16,32,256]{3,2,1,0:T(8,128)S(1)}, f32[4,16,32,256]{3,2,1,0:T(8,128)}, u32[]{:S(2)}) copy-start(f32[4,16,32,256]{3,2,1,0:T(8,128)} %get-tuple-element.9) | copy-start | bytes 6291460
  37.2 39.5 %collective-permute-start = (bf16[4,15,32,256]{3,2,1,0:T(8,128)(2,1)}, bf16[4,15,32,256]{3,2,1,0:T(8,128)(2,1)}, u32[]{:S(2)}, u32[]{:S(2)}) collective-permute-start(bf16[4,15,32,256]{3,2,1,0:T(8,128)(2,1)} %get-tuple-element.10), channel_id=1, source_target_pairs={{0,1},{2,3},{4,5},{6,7},{8,9},{10,11},{12,13},{14,15},{16,17},{18,... | collective-permute-start | bytes 2949128 | tf_op jit(solution)/shard_map/ppermute | solution.py:133
  73.4 26.7 %collective-permute-start.1 = (bf16[4,15,32,256]{3,2,1,0:T(8,128)(2,1)}, bf16[4,15,32,256]{3,2,1,0:T(8,128)(2,1)}, u32[]{:S(2)}, u32[]{:S(2)}) collective-permute-start(bf16[4,15,32,256]{3,2,1,0:T(8,128)(2,1)} %get-tuple-element.12), channel_id=1, source_target_pairs={{0,1},{2,3},{4,5},{6,7},{8,9},{10,11},{12,13},{14,15},{16,17},{18,... | collective-permute-start | bytes 2949128 | tf_op jit(solution)/shard_map/ppermute | solution.py:133
  78.2 21.9 %copy-start.1 = (f32[4,16,32,256]{3,2,1,0:T(8,128)S(1)}, f32[4,16,32,256]{3,2,1,0:T(8,128)}, u32[]{:S(2)}) copy-start(f32[4,16,32,256]{3,2,1,0:T(8,128)} %get-tuple-element.11) | copy-start | bytes 6291460
  101.7 3.0 %copy-start.4 = (bf16[4,1,32,256]{2,3,0,1:T(8,128)(2,1)S(1)}, bf16[4,1,32,256]{2,3,0,1:T(8,128)(2,1)}, u32[]{:S(2)}) copy-start(bf16[4,1,32,256]{2,3,0,1:T(8,128)(2,1)} %copy.80) | copy-start | bytes 196612
  122.1 6.4 %copy-start.7 = (s32[2,512]{1,0:T(2,128)S(1)}, s32[2,512]{1,0:T(2,128)}, u32[]{:S(2)}) copy-start(s32[2,512]{1,0:T(2,128)} %param.7) | copy-start | bytes 12292
  122.1 53.6 %all-to-all-start = ((bf16[2,64,16,512]{3,1,0,2:T(8,128)(2,1)}), bf16[2,64,16,512]{3,1,0,2:T(8,128)(2,1)S(1)}, u32[]{:S(2)}, u32[]{:S(2)}) async-start(bf16[2,64,16,512]{3,1,0,2:T(8,128)(2,1)} %copy.83), calls=%async_computation | async-start | bytes 4194304 | tf_op jit(solution)/shard_map/all_to_all | solution.py:154
  128.4 2.9 %copy-start.8 = (s32[2,10]{1,0:T(2,128)S(1)}, s32[2,10]{1,0:T(2,128)}, u32[]{:S(2)}) copy-start(s32[2,10]{1,0:T(2,128)} %param.8) | copy-start | bytes 244
  176.3 2.3 copy-start
  176.3 26.1 %collective-permute-start.2 = (bf16[2,1024,256]{2,1,0:T(8,128)(2,1)S(1)}, bf16[2,1024,256]{2,1,0:T(8,128)(2,1)S(1)}, u32[]{:S(2)}, u32[]{:S(2)}) collective-permute-start(bf16[2,1024,256]{2,1,0:T(8,128)(2,1)S(1)} %get-tuple-element.31), channel_id=1, source_target_pairs={{0,1},{1,0},{2,3},{3,2},{4,5},{5,4},{6,7},{7,6},{8,9},{9,8},{10,11... | collective-permute-start | bytes 3145736 | tf_op jit(solution)/shard_map/ppermute | solution.py:168
  176.4 47.8 %collective-permute-start.3 = (bf16[2,1024,256]{2,1,0:T(8,128)(2,1)S(1)}, bf16[2,1024,256]{2,1,0:T(8,128)(2,1)S(1)}, u32[]{:S(2)}, u32[]{:S(2)}) collective-permute-start(bf16[2,1024,256]{2,1,0:T(8,128)(2,1)S(1)} %get-tuple-element.32), channel_id=1, source_target_pairs={{0,1},{1,0},{2,3},{3,2},{4,5},{5,4},{6,7},{7,6},{8,9},{9,8},{10,11... | collective-permute-start | bytes 3145736 | tf_op jit(solution)/shard_map/ppermute | solution.py:168
  178.5 1.0 copy-start.6
  179.5 1.0 copy-start.5
  226.2 0.9 copy-start.3
